TPU v7x, 512 devices: a whole 4x4x16 slice. The times are simulated.
512 devices in a mesh: front: 32 (over y, x, core), col: 16 (over z).
Axes of the slice: x: 4, y: 4, z: 16, core: 2. Of those that a mesh axis runs over, the one named last changes fastest.
Arguments:
- cases_one: float32 [192, 6144], P('front', 'col'), may hold values from -6 to 6
- cases_two: float32 [192, 10240], P('front', 'col'), may hold values from -6 to 6
- cases_parent: float32 [192, 16384], P('front', 'col'), may hold values from -6 to 6
- inverse_one: float32 [6144, 6144], P('front', 'col'), may hold values from -0.078125 to 0.078125
- inverse_two: float32 [10240, 10240], P('front', 'col'), may hold values from -0.0625 to 0.0625
- inverse_parent: float32 [16384, 16384], P('front', 'col'), may hold values from -0.046875 to 0.046875
- coupling_one: float32 [6144, 4096], P('front', 'col'), may hold values from -0.078125 to 0.078125
- coupling_two: float32 [10240, 8192], P('front', 'col'), may hold values from -0.0625 to 0.0625
- map_one: int32 [4096], replicated, may hold values from 0 to 16383, as said below
- map_two: int32 [8192], replicated, may hold values from 0 to 16383, as said below
Outputs:
- solution_one: float32 [192, 6144], P('front', 'col')
- solution_two: float32 [192, 10240], P('front', 'col')
- solution_parent: float32 [192, 16384], P('front', 'col')
Inputs may be any that keep to these rules, and one draw needn't show every extreme that they name: `map_one`: entries are distinct. Each aligned block of 256 entries sends the same number of entries into each aligned range of 1024 parent rows. `map_two`: entries are distinct. Each aligned block of 512 entries sends the same number of entries into each aligned range of 1024 parent rows.
All inputs are finite; a program needn't handle non-finite values.
Results may differ from a plain program's by a relative error of at most 0.00013.
Values sent between devices are 32-bit elements; how exact they have to be, the bound alone decides.
A program may use at most 64 MiB of HBM per device.

v0:
```python
import jax
import jax.numpy as jnp
from jax import lax
from jax.sharding import PartitionSpec as P


def rows_term(cases, matrix):
    return lax.dot_general(
        cases,
        matrix,
        (((1,), (1,)), ((), ())),
        precision=lax.Precision.HIGHEST,
        preferred_element_type=jnp.float32,
    )


def split_columns(array, widths):
    pieces = []
    offset = 0
    for width in widths:
        pieces.append(array)
        offset = offset + width
    return pieces


def join_columns(arrays):
    return arrays[0]


def forward_product(matrices, cases_list):
    in_widths = [matrix.shape[1] for matrix in matrices]
    out_widths = [matrix.shape[0] for matrix in matrices]
    cases = join_columns(cases_list)
    blocks = split_columns(lax.all_gather(cases, "front", axis=0, tiled=True), in_widths)
    term = join_columns([rows_term(block, matrix) for block, matrix in zip(blocks, matrices)])
    result = lax.psum_scatter(term, "col", scatter_dimension=0, tiled=True)
    return split_columns(result, out_widths)


def backward_product(matrices, cases_list):
    in_widths = [matrix.shape[0] for matrix in matrices]
    out_widths = [matrix.shape[1] for matrix in matrices]
    cases = join_columns(cases_list)
    whole = lax.all_gather(cases, "col", axis=0, tiled=True)
    blocks = split_columns(whole, in_widths)
    result = lax.psum_scatter(
        join_columns(
            [
                jnp.dot(
                    part_rows,
                    matrix,
                    precision=lax.Precision.HIGHEST,
                    preferred_element_type=jnp.float32,
                )
                for part_rows, matrix in zip(blocks, matrices)
            ]
        ),
        "front",
        scatter_dimension=0,
        tiled=True,
    )
    return split_columns(result, out_widths)


def slot_tables(owner_map, owned, owners, place):
    total = owner_map.shape[0]
    width = total // owners
    share = width // owners
    target = owner_map // owned
    source = jnp.arange(total, dtype=jnp.int32) // width
    marks = (target[:, None] == jnp.arange(owners, dtype=jnp.int32)[None, :]).astype(jnp.int32)
    counted = jnp.cumsum(marks.reshape(owners, width, owners), axis=1).reshape(total, owners)
    ranking = jnp.sum(counted * marks, axis=1) - 1
    outgoing = lax.dynamic_slice_in_dim(target * share + ranking, place * width, width, 0)
    arriving = jnp.where(target == place, source * share + ranking, width)
    landing = jnp.zeros((width,), jnp.int32).at[arriving].set(owner_map % owned, mode="drop")
    return (outgoing, landing)


def send_rows(values):
    return lax.all_to_all(values, "col", split_axis=1, concat_axis=1, tiled=True)


def outgoing_order(outgoing):
    width = outgoing.shape[0]
    return jnp.zeros((width,), jnp.int32).at[outgoing].set(jnp.arange(width, dtype=jnp.int32))


def land_rows(arrived, landing, owned):
    return jnp.zeros((arrived.shape[0], owned), jnp.float32).at[:, landing].add(arrived)


def local(
    cases_one,
    cases_two,
    cases_parent,
    inverse_one,
    inverse_two,
    inverse_parent,
    coupling_one,
    coupling_two,
    map_one,
    map_two,
):
    owners = lax.axis_size("col")
    place = lax.axis_index("col")
    owned = cases_parent.shape[1]
    out_one, land_one = slot_tables(map_one, owned, owners, place)
    out_two, land_two = slot_tables(map_two, owned, owners, place)
    solved_one = forward_product([inverse_one], [cases_one])[0]
    update_one = backward_product([coupling_one], [solved_one])[0]
    arrived_one = send_rows(update_one[:, outgoing_order(out_one)])
    solved_two = forward_product([inverse_two], [cases_two])[0]
    update_two = backward_product([coupling_two], [solved_two])[0]
    arrived_two = send_rows(update_two[:, outgoing_order(out_two)])
    assembled = (
        cases_parent
        - land_rows(arrived_one, land_one, owned)
        - land_rows(arrived_two, land_two, owned)
    )
    solved_parent = forward_product([inverse_parent], [assembled])[0]
    solution_parent = backward_product([inverse_parent], [solved_parent])[0]
    returned_one = send_rows(solution_parent[:, land_one])
    lifted_one = forward_product([coupling_one], [returned_one[:, out_one]])[0]
    solution_one = backward_product([inverse_one], [solved_one - lifted_one])[0]
    returned_two = send_rows(solution_parent[:, land_two])
    lifted_two = forward_product([coupling_two], [returned_two[:, out_two]])[0]
    solution_two = backward_product([inverse_two], [solved_two - lifted_two])[0]
    return (solution_one, solution_two, solution_parent)


def solution(mesh):
    return jax.shard_map(
        local,
        mesh=mesh,
        in_specs=(
            P("front", "col"),
            P("front", "col"),
            P("front", "col"),
            P("front", "col"),
            P("front", "col"),
            P("front", "col"),
            P("front", "col"),
            P("front", "col"),
            P(),
            P(),
        ),
        out_specs=(P("front", "col"), P("front", "col"), P("front", "col")),
        check_vma=False,
    )
```

profile of v0, /device:TPU:1, one launch (start us, length us, event | category | flops | bytes accessed | tf_op | source)
XLA Modules:
  0.0 1010.7 jit_solution(4711777306637551469)
XLA Ops:
  7.2 32.3 %all-gather.4 = f32[32,6,640]{2,1,0:T(8,128)} all-gather(f32[1,6,640]{2,1,0:T(8,128)} %bitcast.145), channel_id=1, replica_groups=mesh['front'=32,'col'=16] {'front'}, dimensions={0}, use_global_device_ids=true | all-gather | bytes 506880 | tf_op jit(solution)/shard_map/all_gather | solution.py:34
  40.7 25.9 %all-gather.2 = f32[32,6,384]{2,1,0:T(8,128)} all-gather(f32[1,6,384]{2,1,0:T(8,128)} %bitcast.146), channel_id=1, replica_groups=mesh['front'=32,'col'=16] {'front'}, dimensions={0}, use_global_device_ids=true | all-gather | bytes 304128 | tf_op jit(solution)/shard_map/all_gather | solution.py:34
  71.8 30.9 %fusion.52 = (f32[16,320]{1,0:T(8,128)S(1)}, f32[16,192]{1,0:T(8,128)S(1)}) fusion(f32[192,320]{1,0:T(8,128)} %fusion.56, f32[192,192]{1,0:T(8,128)S(1)} %fusion.54), kind=kCustom, calls=%all-reduce-scatter.10 | all-reduce-scatter fusion | flops 131073 | bytes 428032
  105.1 4.9 collective-permute-start.1
  112.4 4.9 collective-permute-start.14
  117.9 4.5 collective-permute-start.3
  122.5 18.1 %reduce-window.16 = s32[16,16,4,128]{3,1,2,0:T(8,128)S(1)} reduce-window(s32[16,16,4,128]{3,1,2,0:T(8,128)S(1)} %fusion.10, s32[]{:T(128)} %constant.93.clone.1), window={size=1x1x1x128 pad=0_0x0_0x0_0x127_0}, to_apply=%region_8.9 | reduce-window | flops 16646144 | bytes 1048580 | tf_op jit(solution)/shard_map/reduce-window.2
  142.5 30.4 %scatter_custom_fusion.3 = s32[512]{0:T(512)S(1)} fusion(s32[8192]{0:T(1024)S(1)} %get-tuple-element.18, s32[8192]{0:T(1024)S(1)} %get-tuple-element.17, s32[]{:T(128)} %constant.93.clone.1), kind=kCustom, calls=%fused_computation.105 | custom fusion | bytes 2052 | tf_op jit(solution)/shard_map/scatter | solution.py:76
  176.7 9.1 reduce-window.14
  202.7 21.1 %all-gather.3 = f32[16,12,192]{2,1,0:T(8,128)S(1)} all-gather(f32[1,12,192]{2,1,0:T(8,128)S(1)} %fusion.40), channel_id=1, replica_groups=mesh['front'=32,'col'=16] {'col'}, dimensions={0}, use_global_device_ids=true | all-gather | bytes 156672 | tf_op jit(solution)/shard_map/all_gather | solution.py:44
  227.4 22.5 %all-gather.5 = f32[16,12,320]{2,1,0:T(8,128)S(1)} all-gather(f32[1,12,320]{2,1,0:T(8,128)S(1)} %dynamic-slice_bitcast_fusion.1), channel_id=1, replica_groups=mesh['front'=32,'col'=16] {'col'}, dimensions={0}, use_global_device_ids=true | all-gather | bytes 261120 | tf_op jit(solution)/shard_map/all_gather | solution.py:44
  250.8 88.8 %fusion.50 = (f32[8,512]{1,0:T(8,128)S(1)}, f32[8,256]{1,0:T(8,128)S(1)}) fusion(f32[192,512]{1,0:T(8,128)S(1)} %fusion.57, f32[192,256]{1,0:T(8,128)} %fusion.55), kind=kCustom, calls=%all-reduce-scatter.8 | all-reduce-scatter fusion | flops 196609 | bytes 616448
  344.8 8.7 collective-permute-start.7
  368.4 15.6 %scatter_custom_fusion = s32[256]{0:T(256)S(1)} fusion(s32[4096]{0:T(1024)} %get-tuple-element.20, s32[4096]{0:T(1024)} %get-tuple-element.19, s32[]{:T(128)} %constant.93.clone.1), kind=kCustom, calls=%fused_computation.111 | custom fusion | bytes 1536 | tf_op jit(solution)/shard_map/scatter | solution.py:76
  407.0 8.6 all-to-all-done
  421.7 9.3 all-to-all-done.1
  438.8 24.9 %all-gather.6 = f32[32,6,1024]{2,1,0:T(8,128)S(1)} all-gather(f32[1,6,1024]{2,1,0:T(8,128)S(1)} %copy.67), channel_id=1, replica_groups=mesh['front'=32,'col'=16] {'front'}, dimensions={0}, use_global_device_ids=true | all-gather | bytes 811008 | tf_op jit(solution)/shard_map/all_gather | solution.py:34
  468.0 35.0 %fusion.4 = f32[16,512]{1,0:T(8,128)S(1)} fusion(f32[192,512]{1,0:T(8,128)S(1)} %fusion.58), kind=kCustom, calls=%all-reduce-scatter.4 | all-reduce-scatter fusion | flops 131073 | bytes 428032
  515.8 25.6 %all-gather.7 = f32[16,12,512]{2,1,0:T(8,128)S(1)} all-gather(f32[1,12,512]{2,1,0:T(8,128)S(1)} %dynamic-slice_bitcast_fusion), channel_id=1, replica_groups=mesh['front'=32,'col'=16] {'col'}, dimensions={0}, use_global_device_ids=true | all-gather | bytes 417792 | tf_op jit(solution)/shard_map/all_gather | solution.py:44
  543.0 84.0 %fusion.5 = f32[8,1024]{1,0:T(8,128)S(1)} fusion(f32[192,1024]{1,0:T(8,128)S(1)} %fusion.59), kind=kCustom, calls=%all-reduce-scatter.5 | all-reduce-scatter fusion | flops 262145 | bytes 821248
  632.2 11.8 %collective-permute-start.31 = (f32[8,1024]{1,0:T(8,128)S(1)}, f32[8,1024]{1,0:T(8,128)S(1)}, u32[]{:S(2)}, u32[]{:S(2)}) collective-permute-start(f32[8,1024]{1,0:T(8,128)S(1)} %fusion.5), channel_id=1, source_target_pairs={{0,64},{16,80},{32,96},{48,112},{64,128},{80,144},{96,160},{112,17... | collective-permute-start | bytes 98312
  655.9 8.8 all-to-all-start.2
  666.6 9.7 all-to-all-done.2
  681.4 25.9 %all-gather.8 = f32[32,6,256]{2,1,0:T(8,128)S(1)} all-gather(f32[1,6,256]{2,1,0:T(8,128)S(1)} %copy.71), channel_id=2, replica_groups=mesh['front'=32,'col'=16] {'front'}, dimensions={0}, use_global_device_ids=true | all-gather | bytes 202752 | tf_op jit(solution)/shard_map/all_gather | solution.py:34
  710.4 23.7 %all-gather.10 = f32[32,6,512]{2,1,0:T(8,128)S(1)} all-gather(f32[1,6,512]{2,1,0:T(8,128)S(1)} %copy.75), channel_id=3, replica_groups=mesh['front'=32,'col'=16] {'front'}, dimensions={0}, use_global_device_ids=true | all-gather | bytes 405504 | tf_op jit(solution)/shard_map/all_gather | solution.py:34
  736.8 27.9 %fusion.51 = (f32[16,192]{1,0:T(8,128)S(1)}, f32[16,320]{1,0:T(8,128)S(1)}) fusion(f32[192,192]{1,0:T(8,128)} %fusion.60, f32[192,320]{1,0:T(8,128)S(1)} %fusion.62), kind=kCustom, calls=%all-reduce-scatter.9 | all-reduce-scatter fusion | flops 131073 | bytes 428032
  764.8 4.3 collective-permute-start.38
  775.7 5.5 collective-permute-start.39
  790.7 5.0 collective-permute-start.43
  797.0 20.6 %all-gather.9 = f32[16,12,192]{2,1,0:T(8,128)S(1)} all-gather(f32[1,12,192]{2,1,0:T(8,128)S(1)} %fusion.30), channel_id=1, replica_groups=mesh['front'=32,'col'=16] {'col'}, dimensions={0}, use_global_device_ids=true | all-gather | bytes 156672 | tf_op jit(solution)/shard_map/all_gather | solution.py:44
  824.6 23.0 %all-gather.11 = f32[16,12,320]{2,1,0:T(8,128)S(1)} all-gather(f32[1,12,320]{2,1,0:T(8,128)S(1)} %fusion.27), channel_id=1, replica_groups=mesh['front'=32,'col'=16] {'col'}, dimensions={0}, use_global_device_ids=true | all-gather | bytes 261120 | tf_op jit(solution)/shard_map/all_gather | solution.py:44
  851.7 149.2 %all-reduce.24.cloned.1.call-done = (f32[192,384]{1,0:T(8,128)}, f32[192,640]{1,0:T(8,128)}) async-done(((f32[192,384]{1,0:T(8,128)}, f32[192,640]{1,0:T(8,128)}), (f32[192,384]{1,0:T(8,128)}, f32[192,640]{1,0:T(8,128)})) %all-reduce.24.cloned.1.call-update) | async-done | bytes 786448
  (251 shorter events, 172.7 us)
Async XLA Ops:
  102.7 92.0 %collective-permute-start.2 = (f32[16,192]{1,0:T(8,128)S(1)}, f32[16,192]{1,0:T(8,128)}, u32[]{:S(2)}, u32[]{:S(2)}) collective-permute-start(f32[16,192]{1,0:T(8,128)S(1)} %get-tuple-element.16), channel_id=1, source_target_pairs={{0,3},{1,4},{2,5},{3,6},{4,7},{5,8},{6,9},{7,10},{8,11},{9,12},{10... | collective-permute-start | bytes 36872
  105.1 91.8 %collective-permute-start.1 = (f32[16,192]{1,0:T(8,128)S(1)}, f32[16,192]{1,0:T(8,128)}, u32[]{:S(2)}, u32[]{:S(2)}) collective-permute-start(f32[16,192]{1,0:T(8,128)S(1)} %get-tuple-element.16), channel_id=1, source_target_pairs={{0,2},{1,3},{2,4},{3,5},{4,6},{5,7},{6,8},{7,9},{8,10},{9,11},{10,... | collective-permute-start | bytes 36872
  110.0 88.9 %collective-permute-start = (f32[16,192]{1,0:T(8,128)S(1)}, f32[16,192]{1,0:T(8,128)}, u32[]{:S(2)}, u32[]{:S(2)}) collective-permute-start(f32[16,192]{1,0:T(8,128)S(1)} %get-tuple-element.16), channel_id=1, source_target_pairs={{0,1},{1,2},{2,3},{3,4},{4,5},{5,6},{6,7},{7,8},{8,9},{9,10},{10,1... | collective-permute-start | bytes 36872
  112.4 112.4 %collective-permute-start.14 = (f32[16,320]{1,0:T(8,128)S(1)}, f32[16,320]{1,0:T(8,128)}, u32[]{:S(2)}, u32[]{:S(2)}) collective-permute-start(f32[16,320]{1,0:T(8,128)S(1)} %get-tuple-element.15), channel_id=1, source_target_pairs={{0,3},{1,4},{2,5},{3,6},{4,7},{5,8},{6,9},{7,10},{8,11},{9,12},{10... | collective-permute-start | bytes 61448
  117.9 74.6 %collective-permute-start.3 = (f32[12,192]{1,0:T(8,128)}, f32[12,192]{1,0:T(8,128)}, u32[]{:S(2)}, u32[]{:S(2)}) collective-permute-start(f32[12,192]{1,0:T(8,128)} %slice.32), channel_id=1, source_target_pairs={{0,4},{1,5},{2,6},{3,7},{4,8},{5,9},{6,10},{7,11},{8,12},{9,13},{1... | collective-permute-start | bytes 27656
  192.5 32.3 %collective-permute-start.13 = (f32[16,320]{1,0:T(8,128)S(1)}, f32[16,320]{1,0:T(8,128)S(1)}, u32[]{:S(2)}, u32[]{:S(2)}) collective-permute-start(f32[16,320]{1,0:T(8,128)S(1)} %get-tuple-element.15), channel_id=1, source_target_pairs={{0,2},{1,3},{2,4},{3,5},{4,6},{5,7},{6,8},{7,9},{8,10},{9,11},{10,... | collective-permute-start | bytes 61448
  194.7 30.1 %collective-permute-start.12 = (f32[16,320]{1,0:T(8,128)S(1)}, f32[16,320]{1,0:T(8,128)S(1)}, u32[]{:S(2)}, u32[]{:S(2)}) collective-permute-start(f32[16,320]{1,0:T(8,128)S(1)} %get-tuple-element.15), channel_id=1, source_target_pairs={{0,1},{1,2},{2,3},{3,4},{4,5},{5,6},{6,7},{7,8},{8,9},{9,10},{10,1... | collective-permute-start | bytes 61448
  196.9 27.9 %collective-permute-start.15 = (f32[12,320]{1,0:T(8,128)S(1)}, f32[12,320]{1,0:T(8,128)}, u32[]{:S(2)}, u32[]{:S(2)}) collective-permute-start(f32[12,320]{1,0:T(8,128)S(1)} %slice.34), channel_id=1, source_target_pairs={{0,4},{1,5},{2,6},{3,7},{4,8},{5,9},{6,10},{7,11},{8,12},{9,13},{1... | collective-permute-start | bytes 46088
  343.5 16.5 %collective-permute-start.8 = (f32[8,256]{1,0:T(8,128)S(1)}, f32[8,256]{1,0:T(8,128)S(1)}, u32[]{:S(2)}, u32[]{:S(2)}) collective-permute-start(f32[8,256]{1,0:T(8,128)S(1)} %get-tuple-element.8), channel_id=1, source_target_pairs={{0,80},{16,96},{32,112},{48,128},{64,144},{80,160},{96,176},{112,1... | collective-permute-start | bytes 24584
  344.8 17.7 %collective-permute-start.7 = (f32[8,256]{1,0:T(8,128)S(1)}, f32[8,256]{1,0:T(8,128)S(1)}, u32[]{:S(2)}, u32[]{:S(2)}) collective-permute-start(f32[8,256]{1,0:T(8,128)S(1)} %get-tuple-element.8), channel_id=1, source_target_pairs={{0,64},{16,80},{32,96},{48,112},{64,128},{80,144},{96,160},{112,17... | collective-permute-start | bytes 24584
  354.9 39.6 %collective-permute-start.22 = (f32[8,512]{1,0:T(8,128)S(1)}, f32[8,512]{1,0:T(8,128)S(1)}, u32[]{:S(2)}, u32[]{:S(2)}) collective-permute-start(f32[8,512]{1,0:T(8,128)S(1)} %get-tuple-element.7), channel_id=1, source_target_pairs={{0,112},{16,128},{32,144},{48,160},{64,176},{80,192},{96,208},{112... | collective-permute-start | bytes 49160
  357.4 38.7 %collective-permute-start.21 = (f32[8,512]{1,0:T(8,128)S(1)}, f32[8,512]{1,0:T(8,128)S(1)}, u32[]{:S(2)}, u32[]{:S(2)}) collective-permute-start(f32[8,512]{1,0:T(8,128)S(1)} %get-tuple-element.7), channel_id=1, source_target_pairs={{0,96},{16,112},{32,128},{48,144},{64,160},{80,176},{96,192},{112,... | collective-permute-start | bytes 49160
  360.0 24.0 %collective-permute-start.5 = (f32[8,256]{1,0:T(8,128)S(1)}, f32[8,256]{1,0:T(8,128)S(1)}, u32[]{:S(2)}, u32[]{:S(2)}) collective-permute-start(f32[8,256]{1,0:T(8,128)S(1)} %get-tuple-element.8), channel_id=1, source_target_pairs={{0,32},{16,48},{32,64},{48,80},{64,96},{80,112},{96,128},{112,144}... | collective-permute-start | bytes 24584
  362.5 24.1 %collective-permute-start.4 = (f32[8,256]{1,0:T(8,128)S(1)}, f32[8,256]{1,0:T(8,128)S(1)}, u32[]{:S(2)}, u32[]{:S(2)}) collective-permute-start(f32[8,256]{1,0:T(8,128)S(1)} %get-tuple-element.8), channel_id=1, source_target_pairs={{0,16},{16,32},{32,48},{48,64},{64,80},{80,96},{96,112},{112,128},... | collective-permute-start | bytes 24584
  365.8 24.7 %collective-permute-start.23 = (f32[6,512]{1,0:T(8,128)S(1)}, f32[6,512]{1,0:T(8,128)S(1)}, u32[]{:S(2)}, u32[]{:S(2)}) collective-permute-start(f32[6,512]{1,0:T(8,128)S(1)} %slice.35), channel_id=1, source_target_pairs={{0,128},{16,144},{32,160},{48,176},{64,192},{80,208},{96,224},{112... | collective-permute-start | bytes 36872
  384.0 20.0 %collective-permute-start.20 = (f32[8,512]{1,0:T(8,128)S(1)}, f32[8,512]{1,0:T(8,128)S(1)}, u32[]{:S(2)}, u32[]{:S(2)}) collective-permute-start(f32[8,512]{1,0:T(8,128)S(1)} %get-tuple-element.7), channel_id=1, source_target_pairs={{0,80},{16,96},{32,112},{48,128},{64,144},{80,160},{96,176},{112,1... | collective-permute-start | bytes 49160
  386.6 17.4 %collective-permute-start.19 = (f32[8,512]{1,0:T(8,128)S(1)}, f32[8,512]{1,0:T(8,128)S(1)}, u32[]{:S(2)}, u32[]{:S(2)}) collective-permute-start(f32[8,512]{1,0:T(8,128)S(1)} %get-tuple-element.7), channel_id=1, source_target_pairs={{0,64},{16,80},{32,96},{48,112},{64,128},{80,144},{96,160},{112,17... | collective-permute-start | bytes 49160
  400.0 15.6 %all-to-all-start = ((f32[6,16,16]{2,0,1:T(8,128)}), f32[6,16,16]{2,0,1:T(8,128)S(1)}, u32[]{:S(2)}, u32[]{:S(2)}) async-start(f32[6,16,16]{2,0,1:T(8,128)} %copy.56), calls=%async_computation | async-start | bytes 131072 | tf_op jit(solution)/shard_map/all_to_all | solution.py:81
  627.0 18.4 %collective-permute-start.34 = (f32[8,1024]{1,0:T(8,128)S(1)}, f32[8,1024]{1,0:T(8,128)S(1)}, u32[]{:S(2)}, u32[]{:S(2)}) collective-permute-start(f32[8,1024]{1,0:T(8,128)S(1)} %fusion.5), channel_id=1, source_target_pairs={{0,112},{16,128},{32,144},{48,160},{64,176},{80,192},{96,208},{112... | collective-permute-start | bytes 98312
  628.3 21.1 %collective-permute-start.33 = (f32[8,1024]{1,0:T(8,128)S(1)}, f32[8,1024]{1,0:T(8,128)S(1)}, u32[]{:S(2)}, u32[]{:S(2)}) collective-permute-start(f32[8,1024]{1,0:T(8,128)S(1)} %fusion.5), channel_id=1, source_target_pairs={{0,96},{16,112},{32,128},{48,144},{64,160},{80,176},{96,192},{112,... | collective-permute-start | bytes 98312
  630.9 20.7 %collective-permute-start.32 = (f32[8,1024]{1,0:T(8,128)S(1)}, f32[8,1024]{1,0:T(8,128)S(1)}, u32[]{:S(2)}, u32[]{:S(2)}) collective-permute-start(f32[8,1024]{1,0:T(8,128)S(1)} %fusion.5), channel_id=1, source_target_pairs={{0,80},{16,96},{32,112},{48,128},{64,144},{80,160},{96,176},{112,1... | collective-permute-start | bytes 98312
  632.2 19.4 %collective-permute-start.31 = (f32[8,1024]{1,0:T(8,128)S(1)}, f32[8,1024]{1,0:T(8,128)S(1)}, u32[]{:S(2)}, u32[]{:S(2)}) collective-permute-start(f32[8,1024]{1,0:T(8,128)S(1)} %fusion.5), channel_id=1, source_target_pairs={{0,64},{16,80},{32,96},{48,112},{64,128},{80,144},{96,160},{112,17... | collective-permute-start | bytes 98312
  655.9 20.5 %all-to-all-start.2 = ((f32[6,16,16]{2,0,1:T(8,128)}), f32[6,16,16]{2,0,1:T(8,128)S(1)}, u32[]{:S(2)}, u32[]{:S(2)}) async-start(f32[6,16,16]{2,0,1:T(8,128)} %copy.69), calls=%async_computation.2 | async-start | bytes 131072 | tf_op jit(solution)/shard_map/all_to_all | solution.py:81
  676.4 32.0 %all-to-all-start.3 = ((f32[16,1,192]{2,1,0:T(1,128)}), f32[16,1,192]{2,1,0:T(1,128)S(1)}, u32[]{:S(2)}, u32[]{:S(2)}) async-start(f32[16,1,192]{2,1,0:T(1,128)} %reshape.234), calls=%async_computation.3 | async-start | bytes 32768 | tf_op jit(solution)/shard_map/all_to_all | solution.py:81
  680.3 320.6 %all-reduce.24.cloned.1.call-start = ((), (), s32[]{:S(2)}) async-start(), calls=%async_computation.4 | async-start | bytes 1572864
  764.8 23.7 %collective-permute-start.38 = (f32[16,192]{1,0:T(8,128)S(1)}, f32[16,192]{1,0:T(8,128)S(1)}, u32[]{:S(2)}, u32[]{:S(2)}) collective-permute-start(f32[16,192]{1,0:T(8,128)S(1)} %get-tuple-element.11), channel_id=1, source_target_pairs={{0,3},{1,4},{2,5},{3,6},{4,7},{5,8},{6,9},{7,10},{8,11},{9,12},{10... | collective-permute-start | bytes 36872
  769.1 21.6 %collective-permute-start.37 = (f32[16,192]{1,0:T(8,128)S(1)}, f32[16,192]{1,0:T(8,128)S(1)}, u32[]{:S(2)}, u32[]{:S(2)}) collective-permute-start(f32[16,192]{1,0:T(8,128)S(1)} %get-tuple-element.11), channel_id=1, source_target_pairs={{0,2},{1,3},{2,4},{3,5},{4,6},{5,7},{6,8},{7,9},{8,10},{9,11},{10,... | collective-permute-start | bytes 36872
  772.8 23.0 %collective-permute-start.36 = (f32[16,192]{1,0:T(8,128)S(1)}, f32[16,192]{1,0:T(8,128)S(1)}, u32[]{:S(2)}, u32[]{:S(2)}) collective-permute-start(f32[16,192]{1,0:T(8,128)S(1)} %get-tuple-element.11), channel_id=1, source_target_pairs={{0,1},{1,2},{2,3},{3,4},{4,5},{5,6},{6,7},{7,8},{8,9},{9,10},{10,1... | collective-permute-start | bytes 36872
  781.8 38.7 %collective-permute-start.42 = (f32[16,320]{1,0:T(8,128)S(1)}, f32[16,320]{1,0:T(8,128)}, u32[]{:S(2)}, u32[]{:S(2)}) collective-permute-start(f32[16,320]{1,0:T(8,128)S(1)} %get-tuple-element.12), channel_id=1, source_target_pairs={{0,3},{1,4},{2,5},{3,6},{4,7},{5,8},{6,9},{7,10},{8,11},{9,12},{10... | collective-permute-start | bytes 61448
  785.7 34.7 %collective-permute-start.41 = (f32[16,320]{1,0:T(8,128)S(1)}, f32[16,320]{1,0:T(8,128)}, u32[]{:S(2)}, u32[]{:S(2)}) collective-permute-start(f32[16,320]{1,0:T(8,128)S(1)} %get-tuple-element.12), channel_id=1, source_target_pairs={{0,2},{1,3},{2,4},{3,5},{4,6},{5,7},{6,8},{7,9},{8,10},{9,11},{10,... | collective-permute-start | bytes 61448
  788.5 31.9 %collective-permute-start.40 = (f32[16,320]{1,0:T(8,128)S(1)}, f32[16,320]{1,0:T(8,128)}, u32[]{:S(2)}, u32[]{:S(2)}) collective-permute-start(f32[16,320]{1,0:T(8,128)S(1)} %get-tuple-element.12), channel_id=1, source_target_pairs={{0,1},{1,2},{2,3},{3,4},{4,5},{5,6},{6,7},{7,8},{8,9},{9,10},{10,1... | collective-permute-start | bytes 61448
  790.7 29.7 %collective-permute-start.43 = (f32[12,320]{1,0:T(8,128)}, f32[12,320]{1,0:T(8,128)}, u32[]{:S(2)}, u32[]{:S(2)}) collective-permute-start(f32[12,320]{1,0:T(8,128)} %slice.39), channel_id=1, source_target_pairs={{0,4},{1,5},{2,6},{3,7},{4,8},{5,9},{6,10},{7,11},{8,12},{9,13},{1... | collective-permute-start | bytes 46088
  (38 other events, 2164.7 us)
Sparse Core Ops, SparseCore 0:
  851.3 149.5 all-reduce.23
where the time goes:
time: 1020 us; the launch traced here: 1010 us
  blocking collectives  512 us (50%)
  waiting for transfers between devices  179 us (18%)
  starting transfers between devices  153 us (15%)
  local copies, waits for them, and re-layouts  89.9 us (9%)
  other arithmetic  41.4 us (4%)
  matrix products  18 us (2%)
  between operations  17.4 us (2%)
    unnamed x5, blocking collectives  267 us
    unnamed x46, waiting for transfers between devices  151 us
    all_gather x5, blocking collectives, forward_product(): lax.all_gather(cases, 'front', axis=0, tiled=True)  133 us
    unnamed x45, starting transfers between devices  132 us
    all_gather x5, blocking collectives, backward_product(): whole = lax.all_gather(cases, 'col', axis=0, tiled=True)  113 us
    scatter x2, local copies, waits for them, and re-layouts, slot_tables(): jnp.zeros((width,), jnp.int32).at[arriving]  46.1 us
    unnamed x88, local copies, waits for them, and re-layouts  29.2 us
    another operation x4, other arithmetic  28.1 us
  transfers between devices with their start and end apart: 49, of which 6 were waited for; matrix products, arithmetic and copies ran while one was open for 11% of the time, Pallas kernels for 0%

commit v1 on v0

v1 whole, which is shorter than its diff:
```python
import functools

import jax
import jax.numpy as jnp
from jax import lax
from jax.experimental import pallas as pl
from jax.experimental.pallas import tpu as pltpu
from jax.sharding import PartitionSpec as P

MESH = pl.DeviceIdType.MESH
F32, BF16 = jnp.float32, jnp.bfloat16
CHIPS = [(dy, dx) for dy in range(4) for dx in range(4) if (dy, dx) != (0, 0)]
CHIPS.sort(key=lambda o: -(min(o[0], 4 - o[0]) + min(o[1], 4 - o[1])))
Z_ORDER = sorted(range(1, 16), key=lambda d: -min(d, 16 - d))


def split(value):
    high = value.astype(BF16)
    return high, (value - high.astype(F32)).astype(BF16)


def dot(left, right):
    return lax.dot_general(left, right, (((1,), (0,)), ((), ())), preferred_element_type=F32)


def dot_t(left, right):
    return lax.dot_general(left, right, (((1,), (1,)), ((), ())), preferred_element_type=F32)


def three(dot_fn, left, right):
    (lh, ll), (rh, rl) = left, right
    return dot_fn(lh, rh) + (dot_fn(lh, rl) + dot_fn(ll, rh))


def iota(shape, dim):
    return lax.broadcasted_iota(jnp.int32, shape, dim)


def scratch_plan():
    plan = {}
    vm = lambda *shape: pltpu.VMEM(shape, F32)
    half = lambda *shape: pltpu.VMEM(shape, BF16)
    dma = lambda *shape: pltpu.SemaphoreType.DMA(shape)
    for name, shape in (("io", (192, 384)), ("it", (320, 640)), ("ip", (512, 1024)), ("ko", (192, 256)), ("kt", (320, 512))):
        plan[name] = vm(*shape)
    plan["load"] = dma(5)
    for name in ("wc", "wp", "ck"):
        plan[name + "_h"] = half(512, 1024)
        plan[name + "_l"] = half(512, 1024)
    plan["ka_h"], plan["ka_l"] = half(256, 256), half(256, 256)
    plan["kb_h"], plan["kb_l"] = half(384, 512), half(384, 512)
    plan["sa"], plan["ra"] = vm(16, 16, 256), vm(16, 16, 256)
    plan["sb"], plan["rb"] = vm(16, 32, 384), vm(16, 32, 384)
    plan["sa_s"], plan["sa_r"] = dma(16), dma(16)
    plan["sb_s"], plan["sb_r"] = dma(16), dma(16)
    for i in range(3):
        plan[f"ag{i}"] = vm(16, 8, 1024)
        plan[f"x{i}"] = vm(2, 96, 1024)
        plan[f"ag{i}_s"], plan[f"ag{i}_r"] = dma(16), dma(16)
        plan[f"yp{i}"] = vm(4, 4, 48, 128)
        for n in ("na", "nb", "nc"):
            plan[f"{n}{i}"] = vm(4, 48, 128)
            plan[f"{n}{i}_s"], plan[f"{n}{i}_r"] = dma(4), dma(4)
        plan[f"fs{i}"], plan[f"fr{i}"] = vm(4, 48, 128), vm(4, 48, 128)
        plan[f"fs{i}_s"], plan[f"fs{i}_r"] = dma(4), dma(4)
        plan[f"g{i}"] = vm(4, 4, 48, 128)
        plan[f"gf{i}_s"], plan[f"gf{i}_r"] = dma(4), dma(4)
        for n in ("ga", "gb", "gc"):
            plan[f"{n}{i}_s"], plan[f"{n}{i}_r"] = dma(4), dma(4)
        plan[f"p{i}"] = vm(2, 96, 1024)
        plan[f"cr{i}"] = vm(96, 1024)
        plan[f"rs{i}"], plan[f"rr{i}"] = vm(16, 8, 1024), vm(16, 8, 1024)
        plan[f"rs{i}_s"], plan[f"rs{i}_r"] = dma(16), dma(16)
    return plan


PLAN = scratch_plan()
NAMES = list(PLAN)


def kernel(co, ct, cp, io, it, ip, ko, kt, m1, m2, out1, out2, outp, *scratch):
    r_ = dict(zip(NAMES, scratch))
    f, z = lax.axis_index("front"), lax.axis_index("col")
    core, chip = f % 2, f // 2
    x, y = chip % 4, chip // 4
    sent = []

    def copy(src, dst, send, recv, device):
        c = pltpu.make_async_remote_copy(
            src_ref=src, dst_ref=dst, send_sem=send, recv_sem=recv, device_id=device, device_id_type=MESH
        )
        c.start()
        sent.append(c)
        return c

    def at_chip(offset):
        other = ((y + offset[0]) % 4) * 4 + (x + offset[1]) % 4
        return other, (other * 2 + core, z)

    sibling = (chip * 2 + (1 - core), z)

    def at_z(step):
        return (f, (z + step + 16) % 16)

    loads = {}
    for i, (name, ref) in enumerate((("ko", ko), ("kt", kt), ("io", io), ("it", it), ("ip", ip))):
        loads[name] = pltpu.make_async_copy(ref, r_[name], r_["load"].at[i])
        loads[name].start()

    barrier = pltpu.get_barrier_semaphore()
    pl.semaphore_signal(barrier, inc=1, device_id=sibling, device_id_type=MESH)
    for o in CHIPS:
        pl.semaphore_signal(barrier, inc=1, device_id=at_chip(o)[1], device_id_type=MESH)
    for d in Z_ORDER:
        pl.semaphore_signal(barrier, inc=1, device_id=at_z(d), device_id_type=MESH)

    def sort_columns(mapped, width, source, rows, name):
        share = width // 16
        target = lax.shift_right_logical(mapped, 10)
        position = jnp.bitwise_and(mapped, 1023).astype(F32)
        marks = (iota((16, width), 0) == target).astype(F32)
        below = (iota((width, width), 0) < iota((width, width), 1)).astype(F32).astype(BF16)
        ranking = jnp.sum(dot(marks.astype(BF16), below) * marks, axis=0, keepdims=True)
        place = target * share + ranking.astype(jnp.int32)
        chosen = (iota((width, width), 0) == place).astype(F32).astype(BF16)
        high, low = r_[name + "_h"], r_[name + "_l"]
        high[0:rows, :], low[0:rows, :] = split(source[...])
        tail = jnp.where(iota((64, width), 0) == 0, position, 0.0)
        high[rows : rows + 64, :], low[rows : rows + 64, :] = split(tail)
        return dot_t(chosen, high[...]) + dot_t(chosen, low[...])

    loads["ko"].wait()
    r_["sa"][...] = sort_columns(m1[z], 256, r_["ko"], 192, "ka").reshape(16, 16, 256)
    loads["kt"].wait()
    r_["sb"][...] = sort_columns(m2[z], 512, r_["kt"], 320, "kb").reshape(16, 32, 384)

    ag0 = r_["ag0"]
    pad = jnp.zeros((2, 1024), F32)
    ag0[chip, 0:6, 0:384] = co[...]
    ag0[chip, 0:6, 384:1024] = ct[...]
    ag0[chip, 6:8, :] = pad

    pl.semaphore_wait(barrier, 31)

    def gather_start(i):
        buf = r_[f"ag{i}"]
        return [
            copy(buf.at[chip], buf.at[chip], r_[f"ag{i}_s"].at[k], r_[f"ag{i}_r"].at[k], at_chip(o)[1])
            for k, o in enumerate(CHIPS)
        ]

    def gather_end(i, copies):
        buf, xs = r_[f"ag{i}"], r_[f"x{i}"]
        for c in copies:
            c.wait_recv()
        for j in range(16):
            xs[0, 6 * j : 6 * j + 6, :] = buf[j, 0:6, :]
        copy(xs.at[0], xs.at[1], r_[f"ag{i}_s"].at[15], r_[f"ag{i}_r"].at[15], sibling).wait_recv()
        return xs[...].reshape(192, 1024)

    def share_start(i):
        yp, copies = r_[f"yp{i}"], []
        for o in (2, 1, 3, 0):
            q = (z // 4 + o) % 4
            for n, step in (("na", 1), ("nb", 15), ("nc", 2 + 12 * (q // 2))):
                sem = q
                copies.append(
                    (o, copy(yp.at[(z + step) % 4, q], r_[f"{n}{i}"].at[q], r_[f"{n}{i}_s"].at[sem], r_[f"{n}{i}_r"].at[sem], at_z(step)))
                )
        return copies

    def share_end(i, copies):
        yp, fs, fr, g = r_[f"yp{i}"], r_[f"fs{i}"], r_[f"fr{i}"], r_[f"g{i}"]
        r, q0 = z % 4, z // 4
        far, total = [], None
        for o in (2, 1, 3, 0):
            q = (q0 + o) % 4
            for k, c in copies:
                if k == o:
                    c.wait_recv()
            total = (yp[r, q] + r_[f"na{i}"][q]) + (r_[f"nb{i}"][q] + r_[f"nc{i}"][q])
            if o:
                fs[o] = total
                far.append(copy(fs.at[o], fr.at[o], r_[f"fs{i}_s"].at[o], r_[f"fs{i}_r"].at[o], at_z(4 * o)))
        for c in far:
            c.wait_recv()
        g[r, q0] = (total + fr[1]) + (fr[2] + fr[3])
        far = {
            o: copy(g.at[r, q0], g.at[r, q0], r_[f"gf{i}_s"].at[o], r_[f"gf{i}_r"].at[o], at_z(4 * o)) for o in (2, 1, 3)
        }
        near = []
        for o in (0, 1, 3, 2):
            q = (q0 - o + 4) % 4
            if o:
                far[o].wait_recv()
            for n, step in (("ga", 1), ("gb", 15), ("gc", 2 + 12 * (q // 2))):
                near.append(copy(g.at[r, q], g.at[r, q], r_[f"{n}{i}_s"].at[q], r_[f"{n}{i}_r"].at[q], at_z(step)))
        for c in near:
            c.wait_recv()
        return jnp.concatenate([g[k].reshape(192, 128) for k in range(4)], axis=1)

    def put_rows(i, value):
        for k in range(4):
            r_[f"yp{i}"][k] = value[:, 128 * k : 128 * k + 128].reshape(4, 48, 128)

    def reduce_front(i, value):
        p, cr, rs, rr = r_[f"p{i}"], r_[f"cr{i}"], r_[f"rs{i}"], r_[f"rr{i}"]
        p[...] = value.reshape(2, 96, 1024)
        copy(p.at[1], cr, r_[f"rs{i}_s"].at[15], r_[f"rs{i}_r"].at[15], sibling).wait_recv()
        for j in range(16):
            rs[j, 0:6, :] = p[0, 6 * j : 6 * j + 6, :] + cr[6 * j : 6 * j + 6, :]
            rs[j, 6:8, :] = pad
        copies = [
            copy(rs.at[at_chip(o)[0]], rr.at[k], r_[f"rs{i}_s"].at[k], r_[f"rs{i}_r"].at[k], at_chip(o)[1])
            for k, o in enumerate(CHIPS)
        ]
        total = rs[chip]
        for k, c in enumerate(copies):
            c.wait_recv()
            total = total + rr[k]
        return total

    first = gather_start(0)
    moved = []
    for n, d in enumerate(Z_ORDER):
        to = (z + d) % 16
        for name in ("a", "b"):
            s = r_["s" + name]
            moved.append(copy(s.at[to], r_["r" + name].at[z], r_[f"s{name}_s"].at[n], r_[f"s{name}_r"].at[n], at_z(d)))
    r_["ra"][z] = r_["sa"][z]
    r_["rb"][z] = r_["sb"][z]

    for name in ("wc_h", "wc_l"):
        r_[name][0:192, 384:1024] = jnp.zeros((192, 640), BF16)
        r_[name][192:512, 0:384] = jnp.zeros((320, 384), BF16)
    loads["io"].wait()
    r_["wc_h"][0:192, 0:384], r_["wc_l"][0:192, 0:384] = split(r_["io"][...])
    loads["it"].wait()
    r_["wc_h"][192:512, 384:1024], r_["wc_l"][192:512, 384:1024] = split(r_["it"][...])
    loads["ip"].wait()
    r_["wp_h"][...], r_["wp_l"][...] = split(r_["ip"][...])
    pair = lambda name: (r_[name + "_h"][...], r_[name + "_l"][...])

    cases = gather_end(0, first)
    put_rows(0, three(dot_t, split(cases), pair("wc")))
    near = share_start(0)

    solved = share_end(0, near)

    for c in moved:
        c.wait_recv()
    for name, width, lanes, rows, start in (("ra", 256, 256, 192, 0), ("rb", 512, 384, 320, 192)):
        got = r_[name][...].reshape(width, lanes)
        land = (iota((width, 1024), 1) == got[:, rows : rows + 1].astype(jnp.int32)).astype(F32).astype(BF16)
        high, low = split(got.T)
        r_["ck_h"][start : start + rows, :] = dot(high[0:rows], land).astype(BF16)
        r_["ck_l"][start : start + rows, :] = dot(low[0:rows], land).astype(BF16)

    updated = reduce_front(0, three(dot, split(solved), pair("ck")))

    ag1 = r_["ag1"]
    ag1[chip, 0:6, :] = cp[...] - updated[0:6]
    ag1[chip, 6:8, :] = pad
    assembled = gather_end(1, gather_start(1))
    put_rows(1, three(dot_t, split(assembled), pair("wp")))
    solved_parent = share_end(1, share_start(1))
    parent = reduce_front(1, three(dot, split(solved_parent), pair("wp")))
    outp[...] = parent[0:6]
    r_["ag2"][chip] = parent

    parents = gather_end(2, gather_start(2))
    put_rows(2, three(dot_t, split(parents), pair("ck")))
    lifted = share_end(2, share_start(2))
    solved = jnp.concatenate([r_["g0"][k].reshape(192, 128) for k in range(4)], axis=1)
    last = reduce_front(2, three(dot, split(solved - lifted), pair("wc")))
    out1[...] = last[0:6, 0:384]
    out2[...] = last[0:6, 384:1024]

    for c in sent:
        c.wait_send()


def local(co, ct, cp, io, it, ip, ko, kt, m1, m2):
    vmem, hbm = pl.BlockSpec(memory_space=pltpu.VMEM), pl.BlockSpec(memory_space=pl.ANY)
    shape = lambda like: jax.ShapeDtypeStruct(like.shape, F32)
    return tuple(
        pl.pallas_call(
            kernel,
            name="fronts",
            out_shape=(shape(co), shape(ct), shape(cp)),
            in_specs=[vmem] * 3 + [hbm] * 5 + [vmem] * 2,
            out_specs=(vmem,) * 3,
            scratch_shapes=[PLAN[n] for n in NAMES],
            compiler_params=pltpu.CompilerParams(
                collective_id=1, has_side_effects=True, vmem_limit_bytes=58 * 2**20
            ),
        )(co, ct, cp, io, it, ip, ko, kt, m1.reshape(16, 1, 256), m2.reshape(16, 1, 512))
    )


def solution(mesh):
    block = P("front", "col")
    return jax.shard_map(
        local,
        mesh=mesh,
        in_specs=(block,) * 8 + (P(), P()),
        out_specs=(block,) * 3,
        check_vma=False,
    )
```

time: 1020 us -> 203 us (0.20)
  blocking collectives: 512 us -> 0 us
  Pallas kernels: 0 us -> 198 us
  waiting for transfers between devices: 179 us -> 0 us
  starting transfers between devices: 153 us -> 0 us
  local copies, waits for them, and re-layouts: 89.9 us -> 4.02 us
  other arithmetic: 41.4 us -> 0 us
  matrix products: 18 us -> 0 us
  between operations: 17.4 us -> 0.64 us
    unnamed x5 -> x0, blocking collectives: 267 us -> none
    all_gather x10 -> x0, blocking collectives: 245 us -> none  [the longest x5 133 us: forward_product(): lax.all_gather(cases, 'front', axis=0, tiled=True)]
    pallas_call x0 -> x1, Pallas kernels: none -> 198 us  [local(): pl.pallas_call(kernel, name='fronts', out_shape=(shape(co), shape(ct), sh...]
    unnamed x46 -> x0, waiting for transfers between devices: 151 us -> none
    unnamed x45 -> x0, starting transfers between devices: 132 us -> none
    scatter x4 -> x0, local copies, waits for them, and re-layouts: 49.9 us -> none  [the longest x2 46.1 us: slot_tables(): jnp.zeros((width,), jnp.int32).at[arriving]]
    another operation x4 -> x0, other arithmetic: 28.1 us -> none
    all_to_all x4 -> x0, waiting for transfers between devices: 27.7 us -> none  [send_rows(): lax.all_to_all(values, 'col', split_axis=1, concat_axis=1, tiled=True)]
  transfers between devices with their start and end apart: 49 -> 0, of which waited for: 6 -> 0; matrix products, arithmetic and copies ran while one was open for 11% -> 0% of each run, Pallas kernels for 0% -> 0%
where the time goes in v1:
time: 203 us; the launch traced here: 202 us
  Pallas kernels  198 us (98%)
  local copies, waits for them, and re-layouts  4.02 us (2%)
    pallas_call x1, Pallas kernels, local(): pl.pallas_call(kernel, name='fronts', out_shape=(shape(co), shape(ct), sh...  198 us

profile of v1, /device:TPU:1, one launch (start us, length us, event | category | flops | bytes accessed | tf_op | source)
XLA Modules:
  0.0 202.4 jit_solution(14067936523940258203)
XLA Ops:
  0.6 197.8 %fronts.1 = (f32[6,384]{1,0:T(8,128)}, f32[6,640]{1,0:T(8,128)}, f32[6,1024]{1,0:T(8,128)}) custom-call(f32[6,384]{1,0:T(8,128)} %co.1, f32[6,640]{1,0:T(8,128)} %ct.1, f32[6,1024]{1,0:T(8,128)} %cp.1, f32[192,384]{1,0:T(8,128)} %io.1, f32[320,640]{1,0:T(8,128)} %it.1, f32[512,1024]{1,0:T(8,128)} %ip.1, f32[192,256]{1,0:T(8,128)} %ko.1, f32[320,512]{1,0:T(8,128)} %kt.1, ...), custom_call_target="tpu_custom_call" | custom-call | tf_op jit(solution)/shard_map/fronts/pallas_call | solution.py:287
  198.4 1.3 copy.16
  199.7 1.3 copy.17
  201.0 1.4 copy.18

commit v2 on v1

v2 whole, which is shorter than its diff:
```python
import functools

import jax
import jax.numpy as jnp
from jax import lax
from jax.experimental import pallas as pl
from jax.experimental.pallas import tpu as pltpu
from jax.sharding import PartitionSpec as P

MESH = pl.DeviceIdType.MESH
F32, BF16 = jnp.float32, jnp.bfloat16
CHIPS = [(dy, dx) for dy in range(4) for dx in range(4) if (dy, dx) != (0, 0)]
CHIPS.sort(key=lambda o: -(min(o[0], 4 - o[0]) + min(o[1], 4 - o[1])))
Z_ORDER = sorted(range(1, 16), key=lambda d: -min(d, 16 - d))


def split(value):
    high = value.astype(BF16)
    return high, (value - high.astype(F32)).astype(BF16)


def dot(left, right):
    return lax.dot_general(left, right, (((1,), (0,)), ((), ())), preferred_element_type=F32)


def dot_t(left, right):
    return lax.dot_general(left, right, (((1,), (1,)), ((), ())), preferred_element_type=F32)


def three(dot_fn, left, right):
    (lh, ll), (rh, rl) = left, right
    return dot_fn(lh, rh) + (dot_fn(lh, rl) + dot_fn(ll, rh))


def iota(shape, dim):
    return lax.broadcasted_iota(jnp.int32, shape, dim)


def scratch_plan():
    plan = {}
    vm = lambda *shape: pltpu.VMEM(shape, F32)
    half = lambda *shape: pltpu.VMEM(shape, BF16)
    dma = lambda *shape: pltpu.SemaphoreType.DMA(shape)
    for name, shape in (("io", (192, 384)), ("it", (320, 640)), ("ip", (512, 1024)), ("ko", (192, 256)), ("kt", (320, 512))):
        plan[name] = vm(*shape)
    plan["load"] = dma(5)
    for name, shape in (("wc", (512, 1024)), ("wp", (512, 1024)), ("kc", (512, 768))):
        plan[name + "_h"] = half(*shape)
        plan[name + "_l"] = half(*shape)
    plan["c1"], plan["c2"], plan["land"] = half(256, 256), half(512, 512), half(1024, 768)
    for n in ("ti", "tu", "tb"):
        plan[n], plan[n + "g"] = vm(16, 8, 128), vm(16, 8, 128)
        plan[n + "_s"], plan[n + "_r"] = dma(16), dma(16)
    for i, (there, back) in enumerate(((1024, 768), (1024, 1024), (768, 1024))):
        plan[f"ag{i}"], plan[f"x{i}"] = vm(16, 6, there), vm(2, 96, there)
        plan[f"ag{i}_s"], plan[f"ag{i}_r"] = dma(16), dma(16)
        for h in (0, 1):
            j = f"{i}{h}"
            plan["yp" + j], plan["g" + j] = vm(16, 24, 128), vm(16, 24, 128)
            plan["nr" + j], plan["n3" + j] = vm(4, 3, 24, 128), vm(24, 128)
            plan[f"nr{j}_s"], plan[f"nr{j}_r"] = dma(4, 3), dma(4, 3)
            plan["fs" + j], plan["fr" + j] = vm(3, 24, 128), vm(3, 24, 128)
            plan[f"fs{j}_s"], plan[f"fs{j}_r"] = dma(3), dma(3)
            plan[f"gf{j}_s"], plan[f"gf{j}_r"] = dma(3), dma(3)
            plan[f"gn{j}_s"], plan[f"gn{j}_r"] = dma(4, 3), dma(4, 3)
            plan[f"l{j}_s"], plan[f"l{j}_r"] = dma(2), dma(2)
        plan[f"p{i}"], plan[f"cr{i}"] = vm(2, 96, back), vm(96, back)
        plan[f"rs{i}"], plan[f"rr{i}"] = vm(16, 6, back), vm(16, 6, back)
        plan[f"rs{i}_s"], plan[f"rs{i}_r"] = dma(16), dma(16)
    return plan


PLAN = scratch_plan()
NAMES = list(PLAN)


def kernel(co, ct, cp, io, it, ip, ko, kt, m1, m2, out, *scratch):
    r_ = dict(zip(NAMES, scratch))
    f, z = lax.axis_index("front"), lax.axis_index("col")
    core, chip = f % 2, f // 2
    x, y = chip % 4, chip // 4
    sent = []

    def copy(src, dst, send, recv, device):
        c = pltpu.make_async_remote_copy(
            src_ref=src, dst_ref=dst, send_sem=send, recv_sem=recv, device_id=device, device_id_type=MESH
        )
        c.start()
        sent.append(c)
        return c

    def at_chip(offset):
        other = ((y + offset[0]) % 4) * 4 + (x + offset[1]) % 4
        return other, (other * 2 + core, z)

    sibling = (chip * 2 + (1 - core), z)

    def at_z(step):
        return (f, (z + step + 16) % 16)

    loads = {}
    for i, (name, ref) in enumerate((("ko", ko), ("kt", kt), ("io", io), ("it", it), ("ip", ip))):
        loads[name] = pltpu.make_async_copy(ref, r_[name], r_["load"].at[i])
        loads[name].start()

    barrier = pltpu.get_barrier_semaphore()
    pl.semaphore_signal(barrier, inc=1, device_id=sibling, device_id_type=MESH)
    for o in CHIPS:
        pl.semaphore_signal(barrier, inc=1, device_id=at_chip(o)[1], device_id_type=MESH)
    for d in Z_ORDER:
        pl.semaphore_signal(barrier, inc=1, device_id=at_z(d), device_id_type=MESH)

    def order(mapped, width, name):
        share = width // 16
        target = lax.shift_right_logical(mapped, 10)
        marks = (iota((16, width), 0) == target).astype(F32)
        below = (iota((width, width), 0) < iota((width, width), 1)).astype(F32).astype(BF16)
        ranking = jnp.sum(dot(marks.astype(BF16), below) * marks, axis=0, keepdims=True)
        place = target * share + ranking.astype(jnp.int32)
        r_[name][...] = (iota((width, width), 0) == place).astype(F32).astype(BF16)
        position = jnp.bitwise_and(mapped, 1023).astype(F32)
        return jnp.where(iota((8, width), 0) == 0, position, 0.0)

    def exact(dot_fn, value, name):
        high = value.astype(BF16).astype(F32)
        both = dot_fn(jnp.concatenate([high, value - high], axis=0).astype(BF16), r_[name][...])
        return both[0:8] + both[8:16]

    def exchange(n):
        tiles = r_[n]
        r_[n + "g"][z] = tiles[z]
        return [
            copy(tiles.at[(z + d) % 16], r_[n + "g"].at[z], r_[n + "_s"].at[k], r_[n + "_r"].at[k], at_z(d))
            for k, d in enumerate(Z_ORDER)
        ]

    def to_owners(n, one, two):
        tiles = r_[n]
        for value, name, share, at in ((one, "c1", 16, 0), (two, "c2", 32, 16)):
            ordered = exact(dot_t, value, name)
            for d in range(16):
                tiles[d, :, at : at + share] = ordered[:, share * d : share * d + share]
        return exchange(n)

    def pieces(n, copies, start, stop):
        return jnp.concatenate([r_[n + "g"][k][:, start:stop] for k in range(16)], axis=1)

    ag0 = r_["ag0"]
    ag0[chip, :, 0:384] = co[...]
    ag0[chip, :, 384:1024] = ct[...]
    index_one = order(m1[z], 256, "c1")
    index_two = order(m2[z], 512, "c2")

    pl.semaphore_wait(barrier, 31)

    def gather_start(i):
        buf = r_[f"ag{i}"]
        return [
            copy(buf.at[chip], buf.at[chip], r_[f"ag{i}_s"].at[k], r_[f"ag{i}_r"].at[k], at_chip(o)[1])
            for k, o in enumerate(CHIPS)
        ]

    def gather_end(i, copies):
        buf, xs = r_[f"ag{i}"], r_[f"x{i}"]
        for c in copies:
            c.wait_recv()
        for j in range(16):
            xs[0, 6 * j : 6 * j + 6, :] = buf[j]
        return copy(xs.at[0], xs.at[1], r_[f"ag{i}_s"].at[15], r_[f"ag{i}_r"].at[15], sibling)

    NEAR = (2, 14, 1, 15)
    odd = z % 2
    opposite = 3 - 6 * odd

    def on(t):
        return 15 - 10 * t if not isinstance(t, int) else (0, 5, -5)[t]

    def share_start(i, value):
        yp = r_["yp" + i]
        for k in range(4):
            yp[4 * k : 4 * k + 4] = value[:, 128 * k : 128 * k + 128].reshape(4, 24, 128)
        last = copy(yp.at[(z + 8) % 16], r_["n3" + i], r_[f"l{i}_s"].at[0], r_[f"l{i}_r"].at[0], at_z(opposite))
        near = []
        for t in (1, 2, 0):
            for k, n in enumerate(NEAR):
                near.append(copy(yp.at[(z + n + on(t) + 16) % 16], r_["nr" + i].at[k, t], r_[f"nr{i}_s"].at[k, t], r_[f"nr{i}_r"].at[k, t], at_z(n)))
        return near, last

    def share(i, copies):
        yp, nr, fs, fr, g = r_["yp" + i], r_["nr" + i], r_["fs" + i], r_["fr" + i], r_["g" + i]
        near, last = copies
        yield
        for c in near[:8]:
            c.wait_recv()
        far = []
        for t in (1 + odd, 2 - odd):
            step = on(t)
            total = yp[(z + step + 16) % 16] + ((nr[0, t] + nr[1, t]) + (nr[2, t] + nr[3, t]))
            if far:
                last.wait_recv()
                total = total + r_["n3" + i][...]
            fs[t] = total
            far.append(copy(fs.at[t], fr.at[t], r_[f"fs{i}_s"].at[t], r_[f"fs{i}_r"].at[t], at_z(step)))
        yield
        for c in near[8:]:
            c.wait_recv()
        total = yp[z] + ((nr[0, 0] + nr[1, 0]) + (nr[2, 0] + nr[3, 0]))
        for c in far:
            c.wait_recv()
        g[z] = total + (fr[1] + fr[2])
        far = [copy(g.at[z], g.at[z], r_[f"gf{i}_s"].at[t], r_[f"gf{i}_r"].at[t], at_z(on(t))) for t in (1, 2)]

        def forward(t, block):
            return [
                copy(g.at[block], g.at[block], r_[f"gn{i}_s"].at[k, t], r_[f"gn{i}_r"].at[k, t], at_z(n))
                for k, n in enumerate(NEAR)
            ]

        near = forward(0, z)
        yield
        for c in far:
            c.wait_recv()
        block = (z - on(1 + odd) + 16) % 16
        near.append(copy(g.at[block], g.at[block], r_[f"l{i}_s"].at[1], r_[f"l{i}_r"].at[1], at_z(opposite)))
        for t in (1, 2):
            near += forward(t, (z - on(t) + 16) % 16)
        yield
        for c in near:
            c.wait_recv()

    def shared(i):
        g = r_["g" + i]
        return jnp.concatenate([g[4 * k : 4 * k + 4].reshape(96, 128) for k in range(4)], axis=1)

    def stage(i, first, there, meanwhile, take, back):
        xs, p, cr, rs, rr = r_[f"x{i}"], r_[f"p{i}"], r_[f"cr{i}"], r_[f"rs{i}"], r_[f"rr{i}"]
        across = gather_end(i, first)
        left = share(f"{i}0", share_start(f"{i}0", there(xs[0])))
        next(left)
        across.wait_recv()
        right = share(f"{i}1", share_start(f"{i}1", there(xs[1])))
        meanwhile()
        next(right)
        for _ in range(3):
            next(left)
            next(right)
        for _ in left:
            pass
        p[0] = back(take(shared(f"{i}0"), 0))
        for _ in right:
            pass
        p[1] = back(take(shared(f"{i}1"), 1))
        copy(p.at[1], cr, r_[f"rs{i}_s"].at[15], r_[f"rs{i}_r"].at[15], sibling).wait_recv()
        for j in range(16):
            rs[j] = p[0, 6 * j : 6 * j + 6, :] + cr[6 * j : 6 * j + 6, :]
        copies = [
            copy(rs.at[at_chip(o)[0]], rr.at[k], r_[f"rs{i}_s"].at[k], r_[f"rs{i}_r"].at[k], at_chip(o)[1])
            for k, o in enumerate(CHIPS)
        ]
        total = rs[chip]
        for k, c in enumerate(copies):
            c.wait_recv()
            total = total + rr[k]
        return total

    first = gather_start(0)
    indices = to_owners("ti", index_one, index_two)
    pair = lambda name: (r_[name + "_h"][...], r_[name + "_l"][...])
    product = lambda dot_fn, name: lambda value: three(dot_fn, split(value), pair(name))
    eight = lambda value: jnp.concatenate([value, jnp.zeros((2, value.shape[1]), F32)], axis=0)

    for name in ("wc_h", "wc_l"):
        r_[name][0:192, 384:1024] = jnp.zeros((192, 640), BF16)
        r_[name][192:512, 0:384] = jnp.zeros((320, 384), BF16)
    loads["io"].wait()
    r_["wc_h"][0:192, 0:384], r_["wc_l"][0:192, 0:384] = split(r_["io"][...])
    loads["it"].wait()
    r_["wc_h"][192:512, 384:1024], r_["wc_l"][192:512, 384:1024] = split(r_["it"][...])

    def prepare():
        loads["ko"].wait()
        loads["kt"].wait()
        r_["kc_h"][0:192, 0:256], r_["kc_l"][0:192, 0:256] = split(r_["ko"][...])
        r_["kc_h"][192:512, 256:768], r_["kc_l"][192:512, 256:768] = split(r_["kt"][...])
        for n in ("kc_h", "kc_l"):
            r_[n][0:192, 256:768] = jnp.zeros((192, 512), BF16)
            r_[n][192:512, 0:256] = jnp.zeros((320, 256), BF16)

    updated = stage(0, first, product(dot_t, "wc"), prepare, lambda value, h: value, product(dot, "kc"))
    moved = to_owners("tu", eight(updated[:, 0:256]), eight(updated[:, 256:768]))
    for c in indices:
        c.wait_recv()
    landing = pieces("ti", indices, 0, 48)
    r_["land"][...] = (iota((1024, 768), 0) == landing[0:1, :].astype(jnp.int32)).astype(F32).astype(BF16)
    for c in moved:
        c.wait_recv()
    arrived = exact(dot_t, pieces("tu", moved, 0, 48), "land")

    r_["ag1"][chip] = cp[...] - arrived[0:6]
    first = gather_start(1)
    loads["ip"].wait()
    r_["wp_h"][...], r_["wp_l"][...] = split(r_["ip"][...])
    parent = stage(1, first, product(dot_t, "wp"), lambda: None, lambda value, h: value, product(dot, "wp"))
    out[:, 1024:2048] = parent

    picked = exact(dot, eight(parent), "land")
    for d in range(16):
        r_["tb"][d, :, 0:48] = picked[:, 48 * d : 48 * d + 48]
    moved = exchange("tb")
    for c in moved:
        c.wait_recv()
    r_["ag2"][chip, :, 0:256] = exact(dot, pieces("tb", moved, 0, 16), "c1")[0:6]
    r_["ag2"][chip, :, 256:768] = exact(dot, pieces("tb", moved, 16, 48), "c2")[0:6]
    first = gather_start(2)
    reduced = lambda value, h: shared(f"0{h}") - value
    out[:, 0:1024] = stage(2, first, product(dot_t, "kc"), lambda: None, reduced, product(dot, "wc"))

    for c in sent:
        c.wait_send()


def local(co, ct, cp, io, it, ip, ko, kt, m1, m2):
    vmem, hbm = pl.BlockSpec(memory_space=pltpu.VMEM), pl.BlockSpec(memory_space=pl.ANY)
    whole = pl.pallas_call(
        kernel,
        name="fronts",
        out_shape=jax.ShapeDtypeStruct((6, 2048), F32),
        in_specs=[vmem] * 3 + [hbm] * 5 + [vmem] * 2,
        out_specs=vmem,
        scratch_shapes=[PLAN[n] for n in NAMES],
        compiler_params=pltpu.CompilerParams(collective_id=1, has_side_effects=True, vmem_limit_bytes=58 * 2**20),
    )(co, ct, cp, io, it, ip, ko, kt, m1.reshape(16, 1, 256), m2.reshape(16, 1, 512))
    return whole[:, 0:384], whole[:, 384:1024], whole[:, 1024:2048]


def solution(mesh):
    block = P("front", "col")
    return jax.shard_map(
        local,
        mesh=mesh,
        in_specs=(block,) * 8 + (P(), P()),
        out_specs=(block,) * 3,
        check_vma=False,
    )
```

time: 203 us -> 173 us (0.85)
  Pallas kernels: 198 us -> 168 us
    pallas_call x1, Pallas kernels: 198 us -> 168 us  [local(): pl.pallas_call(kernel, name='fronts', out_shape=jax.ShapeDtypeStruct((6,...]
    slice x0 -> x3, local copies, waits for them, and re-layouts: none -> 4.02 us  [local(): return (whole[:, 0:384], whole[:, 384:1024], whole[:, 1024:2048])]
    unnamed x3 -> x0, local copies, waits for them, and re-layouts: 4.02 us -> none
where the time goes in v2:
time: 173 us; the launch traced here: 172 us
  Pallas kernels  168 us (97%)
  local copies, waits for them, and re-layouts  4.02 us (2%)
    pallas_call x1, Pallas kernels, local(): pl.pallas_call(kernel, name='fronts', out_shape=jax.ShapeDtypeStruct((6,...  168 us
    slice x3, local copies, waits for them, and re-layouts, local(): return (whole[:, 0:384], whole[:, 384:1024], whole[:, 1024:2048])  4.02 us

profile of v2, /device:TPU:1, one launch (start us, length us, event | category | flops | bytes accessed | tf_op | source)
XLA Modules:
  0.0 172.2 jit_solution(8962377765563184409)
XLA Ops:
  0.6 167.5 %fronts.1 = f32[6,2048]{1,0:T(8,128)} custom-call(f32[6,384]{1,0:T(8,128)} %co.1, f32[6,640]{1,0:T(8,128)} %ct.1, f32[6,1024]{1,0:T(8,128)} %cp.1, f32[192,384]{1,0:T(8,128)} %io.1, f32[320,640]{1,0:T(8,128)} %it.1, f32[512,1024]{1,0:T(8,128)} %ip.1, f32[192,256]{1,0:T(8,128)} %ko.1, f32[320,512]{1,0:T(8,128)} %kt.1, s32[16,1,256]{2,1,0:T(1,128)} %bitcast.3, ...), custom_call_target="tpu_custom_call" | custom-call | tf_op jit(solution)/shard_map/fronts/pallas_call | solution.py:324
  168.2 1.3 slice.9
  169.5 1.3 slice.10
  170.8 1.4 slice.11

commit v3 on v2

--- a/solution.py
+++ b/solution.py
@@ -29,7 +29,9 @@
 
 def three(dot_fn, left, right):
     (lh, ll), (rh, rl) = left, right
-    return dot_fn(lh, rh) + (dot_fn(lh, rl) + dot_fn(ll, rh))
+    rows = lh.shape[0]
+    both = dot_fn(jnp.concatenate([lh, ll], axis=0), rh)
+    return both[0:rows] + (both[rows : 2 * rows] + dot_fn(lh, rl))
 
 
 def iota(shape, dim):
@@ -43,7 +45,8 @@
     dma = lambda *shape: pltpu.SemaphoreType.DMA(shape)
     for name, shape in (("io", (192, 384)), ("it", (320, 640)), ("ip", (512, 1024)), ("ko", (192, 256)), ("kt", (320, 512))):
         plan[name] = vm(*shape)
-    plan["load"] = dma(5)
+    plan["cp"], plan["m1"], plan["m2"] = vm(6, 1024), pltpu.VMEM((1, 256), jnp.int32), pltpu.VMEM((1, 512), jnp.int32)
+    plan["load"] = dma(10)
     for name, shape in (("wc", (512, 1024)), ("wp", (512, 1024)), ("kc", (512, 768))):
         plan[name + "_h"] = half(*shape)
         plan[name + "_l"] = half(*shape)
@@ -57,16 +60,15 @@
         for h in (0, 1):
             j = f"{i}{h}"
             plan["yp" + j], plan["g" + j] = vm(16, 24, 128), vm(16, 24, 128)
-            plan["nr" + j], plan["n3" + j] = vm(4, 3, 24, 128), vm(24, 128)
-            plan[f"nr{j}_s"], plan[f"nr{j}_r"] = dma(4, 3), dma(4, 3)
-            plan["fs" + j], plan["fr" + j] = vm(3, 24, 128), vm(3, 24, 128)
-            plan[f"fs{j}_s"], plan[f"fs{j}_r"] = dma(3), dma(3)
-            plan[f"gf{j}_s"], plan[f"gf{j}_r"] = dma(3), dma(3)
-            plan[f"gn{j}_s"], plan[f"gn{j}_r"] = dma(4, 3), dma(4, 3)
-            plan[f"l{j}_s"], plan[f"l{j}_r"] = dma(2), dma(2)
+            plan["ns" + j], plan["nr" + j], plan["n3" + j] = vm(4, 3, 24, 128), vm(4, 3, 24, 128), vm(24, 128)
+            plan["fs" + j], plan["f5" + j], plan["f10" + j] = vm(3, 24, 128), vm(2, 2, 24, 128), vm(2, 24, 128)
+            plan["gs" + j], plan["gr" + j] = vm(3, 24, 128), vm(4, 3, 24, 128)
+            for n, count in (("n", 5), ("f", 4), ("b", 5)):
+                plan[f"{n}{j}_s"], plan[f"{n}{j}_r"] = dma(count), dma(count)
         plan[f"p{i}"], plan[f"cr{i}"] = vm(2, 96, back), vm(96, back)
         plan[f"rs{i}"], plan[f"rr{i}"] = vm(16, 6, back), vm(16, 6, back)
         plan[f"rs{i}_s"], plan[f"rs{i}_r"] = dma(16), dma(16)
+        plan[f"cr{i}_s"], plan[f"cr{i}_r"] = dma(4), dma(4)
     return plan
 
 
@@ -93,15 +95,11 @@
         other = ((y + offset[0]) % 4) * 4 + (x + offset[1]) % 4
         return other, (other * 2 + core, z)
 
+    pair = lambda name: (r_[name + "_h"][...], r_[name + "_l"][...])
     sibling = (chip * 2 + (1 - core), z)
 
     def at_z(step):
         return (f, (z + step + 16) % 16)
-
-    loads = {}
-    for i, (name, ref) in enumerate((("ko", ko), ("kt", kt), ("io", io), ("it", it), ("ip", ip))):
-        loads[name] = pltpu.make_async_copy(ref, r_[name], r_["load"].at[i])
-        loads[name].start()
 
     barrier = pltpu.get_barrier_semaphore()
     pl.semaphore_signal(barrier, inc=1, device_id=sibling, device_id_type=MESH)
@@ -109,6 +107,25 @@
         pl.semaphore_signal(barrier, inc=1, device_id=at_chip(o)[1], device_id_type=MESH)
     for d in Z_ORDER:
         pl.semaphore_signal(barrier, inc=1, device_id=at_z(d), device_id_type=MESH)
+
+    loads = {}
+    ag0 = r_["ag0"]
+    for i, (name, ref, to) in enumerate(
+        (
+            ("co", co, ag0.at[chip, :, 0:384]),
+            ("ct", ct, ag0.at[chip, :, 384:1024]),
+            ("m1", m1.at[z], r_["m1"]),
+            ("m2", m2.at[z], r_["m2"]),
+            ("io", io, r_["io"]),
+            ("it", it, r_["it"]),
+            ("ko", ko, r_["ko"]),
+            ("kt", kt, r_["kt"]),
+            ("cp", cp, r_["cp"]),
+            ("ip", ip, r_["ip"]),
+        )
+    ):
+        loads[name] = pltpu.make_async_copy(ref, to, r_["load"].at[i])
+        loads[name].start()
 
     def order(mapped, width, name):
         share = width // 16
@@ -145,11 +162,12 @@
     def pieces(n, copies, start, stop):
         return jnp.concatenate([r_[n + "g"][k][:, start:stop] for k in range(16)], axis=1)
 
-    ag0 = r_["ag0"]
-    ag0[chip, :, 0:384] = co[...]
-    ag0[chip, :, 384:1024] = ct[...]
-    index_one = order(m1[z], 256, "c1")
-    index_two = order(m2[z], 512, "c2")
+    loads["m1"].wait()
+    loads["m2"].wait()
+    index_one = order(r_["m1"][...], 256, "c1")
+    index_two = order(r_["m2"][...], 512, "c2")
+    loads["co"].wait()
+    loads["ct"].wait()
 
     pl.semaphore_wait(barrier, 31)
 
@@ -172,61 +190,55 @@
     odd = z % 2
     opposite = 3 - 6 * odd
 
-    def on(t):
-        return 15 - 10 * t if not isinstance(t, int) else (0, 5, -5)[t]
+    def block(step, j):
+        return (z + step + 5 * (j - 1) + 32) % 16
 
     def share_start(i, value):
         yp = r_["yp" + i]
         for k in range(4):
             yp[4 * k : 4 * k + 4] = value[:, 128 * k : 128 * k + 128].reshape(4, 24, 128)
-        last = copy(yp.at[(z + 8) % 16], r_["n3" + i], r_[f"l{i}_s"].at[0], r_[f"l{i}_r"].at[0], at_z(opposite))
-        near = []
-        for t in (1, 2, 0):
-            for k, n in enumerate(NEAR):
-                near.append(copy(yp.at[(z + n + on(t) + 16) % 16], r_["nr" + i].at[k, t], r_[f"nr{i}_s"].at[k, t], r_[f"nr{i}_r"].at[k, t], at_z(n)))
-        return near, last
-
-    def share(i, copies):
-        yp, nr, fs, fr, g = r_["yp" + i], r_["nr" + i], r_["fs" + i], r_["fr" + i], r_["g" + i]
-        near, last = copies
+        ns, nr = r_["ns" + i], r_["nr" + i]
+        sems = lambda k: (r_[f"n{i}_s"].at[k], r_[f"n{i}_r"].at[k])
+        near = [copy(yp.at[(z + 8) % 16], r_["n3" + i], *sems(4), at_z(opposite))]
+        for k, n in enumerate(NEAR):
+            for j in range(3):
+                ns[k, j] = yp[block(n, j)]
+            near.append(copy(ns.at[k], nr.at[k], *sems(k), at_z(n)))
+        return near
+
+    def share(i, near):
+        yp, nr, fs, f5, f10 = r_["yp" + i], r_["nr" + i], r_["fs" + i], r_["f5" + i], r_["f10" + i]
+        g, gs, gr = r_["g" + i], r_["gs" + i], r_["gr" + i]
         yield
-        for c in near[:8]:
-            c.wait_recv()
-        far = []
-        for t in (1 + odd, 2 - odd):
-            step = on(t)
-            total = yp[(z + step + 16) % 16] + ((nr[0, t] + nr[1, t]) + (nr[2, t] + nr[3, t]))
-            if far:
-                last.wait_recv()
-                total = total + r_["n3" + i][...]
-            fs[t] = total
-            far.append(copy(fs.at[t], fr.at[t], r_[f"fs{i}_s"].at[t], r_[f"fs{i}_r"].at[t], at_z(step)))
-        yield
-        for c in near[8:]:
-            c.wait_recv()
-        total = yp[z] + ((nr[0, 0] + nr[1, 0]) + (nr[2, 0] + nr[3, 0]))
-        for c in far:
-            c.wait_recv()
-        g[z] = total + (fr[1] + fr[2])
-        far = [copy(g.at[z], g.at[z], r_[f"gf{i}_s"].at[t], r_[f"gf{i}_r"].at[t], at_z(on(t))) for t in (1, 2)]
-
-        def forward(t, block):
-            return [
-                copy(g.at[block], g.at[block], r_[f"gn{i}_s"].at[k, t], r_[f"gn{i}_r"].at[k, t], at_z(n))
-                for k, n in enumerate(NEAR)
-            ]
-
-        near = forward(0, z)
+        for c in near:
+            c.wait_recv()
+        for j in range(3):
+            fs[j] = yp[block(0, j)] + ((nr[0, j] + nr[1, j]) + (nr[2, j] + nr[3, j]))
+        fs[2 * odd] = fs[2 * odd] + r_["n3" + i][...]
+        sems = lambda k: (r_[f"f{i}_s"].at[k], r_[f"f{i}_r"].at[k])
+        far = [
+            copy(fs.at[2], f10.at[0], *sems(0), at_z(10)),
+            copy(fs.at[0], f10.at[1], *sems(1), at_z(-10)),
+            copy(fs.at[pl.ds(1, 2)], f5.at[0], *sems(2), at_z(5)),
+            copy(fs.at[pl.ds(0, 2)], f5.at[1], *sems(3), at_z(-5)),
+        ]
         yield
         for c in far:
             c.wait_recv()
-        block = (z - on(1 + odd) + 16) % 16
-        near.append(copy(g.at[block], g.at[block], r_[f"l{i}_s"].at[1], r_[f"l{i}_r"].at[1], at_z(opposite)))
-        for t in (1, 2):
-            near += forward(t, (z - on(t) + 16) % 16)
+        gs[0] = fs[0] + (f5[0, 0] + f10[0])
+        gs[1] = fs[1] + (f5[0, 1] + f5[1, 0])
+        gs[2] = fs[2] + (f5[1, 1] + f10[1])
+        sent_sems = lambda k: (r_[f"b{i}_s"].at[k], r_[f"b{i}_r"].at[k])
+        near = [copy(gs.at[2 * odd], g.at[block(0, 2 * odd)], *sent_sems(4), at_z(opposite))]
+        near += [copy(gs, gr.at[k], *sent_sems(k), at_z(n)) for k, n in enumerate(NEAR)]
+        for j in range(3):
+            g[block(0, j)] = gs[j]
         yield
         for c in near:
             c.wait_recv()
+        for k, n in enumerate(NEAR):
+            for j in range(3):
+                g[block(-n, j)] = gr[k, j]
 
     def shared(i):
         g = r_["g" + i]
@@ -241,16 +253,21 @@
         right = share(f"{i}1", share_start(f"{i}1", there(xs[1])))
         meanwhile()
         next(right)
-        for _ in range(3):
+        for _ in range(2):
             next(left)
             next(right)
         for _ in left:
             pass
-        p[0] = back(take(shared(f"{i}0"), 0))
+        p[0] = three(dot, split(take(shared(f"{i}0"), 0)), pair(back))
         for _ in right:
             pass
-        p[1] = back(take(shared(f"{i}1"), 1))
-        copy(p.at[1], cr, r_[f"rs{i}_s"].at[15], r_[f"rs{i}_r"].at[15], sibling).wait_recv()
+        value, across = split(take(shared(f"{i}1"), 1)), []
+        for c in range(p.shape[2] // 256):
+            part = (slice(None), slice(256 * c, 256 * c + 256))
+            p[(1,) + part] = three(dot, value, (r_[back + "_h"][part], r_[back + "_l"][part]))
+            across.append(copy(p.at[(1,) + part], cr.at[part], r_[f"cr{i}_s"].at[c], r_[f"cr{i}_r"].at[c], sibling))
+        for c in across:
+            c.wait_recv()
         for j in range(16):
             rs[j] = p[0, 6 * j : 6 * j + 6, :] + cr[6 * j : 6 * j + 6, :]
         copies = [
@@ -265,7 +282,6 @@
 
     first = gather_start(0)
     indices = to_owners("ti", index_one, index_two)
-    pair = lambda name: (r_[name + "_h"][...], r_[name + "_l"][...])
     product = lambda dot_fn, name: lambda value: three(dot_fn, split(value), pair(name))
     eight = lambda value: jnp.concatenate([value, jnp.zeros((2, value.shape[1]), F32)], axis=0)
 
@@ -286,7 +302,7 @@
             r_[n][0:192, 256:768] = jnp.zeros((192, 512), BF16)
             r_[n][192:512, 0:256] = jnp.zeros((320, 256), BF16)
 
-    updated = stage(0, first, product(dot_t, "wc"), prepare, lambda value, h: value, product(dot, "kc"))
+    updated = stage(0, first, product(dot_t, "wc"), prepare, lambda value, h: value, "kc")
     moved = to_owners("tu", eight(updated[:, 0:256]), eight(updated[:, 256:768]))
     for c in indices:
         c.wait_recv()
@@ -296,11 +312,12 @@
         c.wait_recv()
     arrived = exact(dot_t, pieces("tu", moved, 0, 48), "land")
 
-    r_["ag1"][chip] = cp[...] - arrived[0:6]
+    loads["cp"].wait()
+    r_["ag1"][chip] = r_["cp"][...] - arrived[0:6]
     first = gather_start(1)
     loads["ip"].wait()
     r_["wp_h"][...], r_["wp_l"][...] = split(r_["ip"][...])
-    parent = stage(1, first, product(dot_t, "wp"), lambda: None, lambda value, h: value, product(dot, "wp"))
+    parent = stage(1, first, product(dot_t, "wp"), lambda: None, lambda value, h: value, "wp")
     out[:, 1024:2048] = parent
 
     picked = exact(dot, eight(parent), "land")
@@ -313,24 +330,37 @@
     r_["ag2"][chip, :, 256:768] = exact(dot, pieces("tb", moved, 16, 48), "c2")[0:6]
     first = gather_start(2)
     reduced = lambda value, h: shared(f"0{h}") - value
-    out[:, 0:1024] = stage(2, first, product(dot_t, "kc"), lambda: None, reduced, product(dot, "wc"))
+    out[:, 0:1024] = stage(2, first, product(dot_t, "kc"), lambda: None, reduced, "wc")
 
     for c in sent:
         c.wait_send()
 
 
+def parts(whole, one, two, parent):
+    one[...] = whole[:, 0:384]
+    two[...] = whole[:, 384:1024]
+    parent[...] = whole[:, 1024:2048]
+
+
 def local(co, ct, cp, io, it, ip, ko, kt, m1, m2):
     vmem, hbm = pl.BlockSpec(memory_space=pltpu.VMEM), pl.BlockSpec(memory_space=pl.ANY)
+    shape = lambda like: jax.ShapeDtypeStruct(like.shape, F32)
     whole = pl.pallas_call(
         kernel,
         name="fronts",
         out_shape=jax.ShapeDtypeStruct((6, 2048), F32),
-        in_specs=[vmem] * 3 + [hbm] * 5 + [vmem] * 2,
+        in_specs=[hbm] * 10,
         out_specs=vmem,
         scratch_shapes=[PLAN[n] for n in NAMES],
         compiler_params=pltpu.CompilerParams(collective_id=1, has_side_effects=True, vmem_limit_bytes=58 * 2**20),
     )(co, ct, cp, io, it, ip, ko, kt, m1.reshape(16, 1, 256), m2.reshape(16, 1, 512))
-    return whole[:, 0:384], whole[:, 384:1024], whole[:, 1024:2048]
+    return pl.pallas_call(
+        parts,
+        name="parts",
+        out_shape=(shape(co), shape(ct), shape(cp)),
+        in_specs=[vmem],
+        out_specs=(vmem,) * 3,
+    )(whole)
 
 
 def solution(mesh):

time: 173 us -> 165 us (0.954)
  local copies, waits for them, and re-layouts: 4.02 us -> 0 us
  Pallas kernels: 168 us -> 165 us
    pallas_call x1, Pallas kernels: 168 us -> 163 us  [local(): pl.pallas_call(kernel, name='fronts', out_shape=jax.ShapeDtypeStruct((6,...]
    slice x3 -> x0, local copies, waits for them, and re-layouts: 4.02 us -> none  [local(): return (whole[:, 0:384], whole[:, 384:1024], whole[:, 1024:2048])]
where the time goes in v3:
time: 165 us
  Pallas kernels  165 us (100%)
    pallas_call x1, Pallas kernels, local(): pl.pallas_call(kernel, name='fronts', out_shape=jax.ShapeDtypeStruct((6,...  163 us

profile of v3, /device:TPU:1, one launch (start us, length us, event | category | flops | bytes accessed | tf_op | source)
XLA Modules:
  0.0 165.2 jit_solution(11381943926597130625)
XLA Ops:
  0.6 163.1 %fronts.1.whole = f32[6,2048]{1,0:T(8,128)} custom-call(f32[6,384]{1,0:T(8,128)} %co.1, f32[6,640]{1,0:T(8,128)} %ct.1, f32[6,1024]{1,0:T(8,128)} %cp.1, f32[192,384]{1,0:T(8,128)} %io.1, f32[320,640]{1,0:T(8,128)} %it.1, f32[512,1024]{1,0:T(8,128)} %ip.1, f32[192,256]{1,0:T(8,128)} %ko.1, f32[320,512]{1,0:T(8,128)} %kt.1, s32[16,1,256]{2,1,0:T(1,128)} %bitcast.3, ...), custom_call_target="tpu_custom_call" | custom-call | tf_op jit(solution)/shard_map/fronts/pallas_call | solution.py:348
  163.8 1.5 parts.1

commit v4 on v3

--- a/solution.py
+++ b/solution.py
@@ -36,6 +36,10 @@
 
 def iota(shape, dim):
     return lax.broadcasted_iota(jnp.int32, shape, dim)
+
+
+COLUMNS = {"wc": ((0, 1024), (384, 1024)), "kc": ((0, 768), (256, 768)), "wp": ((0, 1024), (0, 1024))}
+ROWS = {"wc": ((0, 256), (0, 512), (128, 512), (128, 512)), "kc": ((0, 256), (128, 512), (128, 512)), "wp": ((0, 512),) * 4}
 
 
 def scratch_plan():
@@ -95,7 +99,12 @@
         other = ((y + offset[0]) % 4) * 4 + (x + offset[1]) % 4
         return other, (other * 2 + core, z)
 
-    pair = lambda name: (r_[name + "_h"][...], r_[name + "_l"][...])
+    def product(dot_fn, left, name, n):
+        start, stop = (ROWS if dot_fn is dot else COLUMNS)[name][n]
+        inner, outer = slice(start, stop), slice(256 * n, 256 * n + 256)
+        at = (inner, outer) if dot_fn is dot else (outer, inner)
+        return three(dot_fn, (left[0][:, inner], left[1][:, inner]), (r_[name + "_h"][at], r_[name + "_l"][at]))
+
     sibling = (chip * 2 + (1 - core), z)
 
     def at_z(step):
@@ -162,10 +171,6 @@
     def pieces(n, copies, start, stop):
         return jnp.concatenate([r_[n + "g"][k][:, start:stop] for k in range(16)], axis=1)
 
-    loads["m1"].wait()
-    loads["m2"].wait()
-    index_one = order(r_["m1"][...], 256, "c1")
-    index_two = order(r_["m2"][...], 512, "c2")
     loads["co"].wait()
     loads["ct"].wait()
 
@@ -246,11 +251,15 @@
 
     def stage(i, first, there, meanwhile, take, back):
         xs, p, cr, rs, rr = r_[f"x{i}"], r_[f"p{i}"], r_[f"cr{i}"], r_[f"rs{i}"], r_[f"rr{i}"]
+        def forth(value):
+            value = split(value)
+            return jnp.concatenate([product(dot_t, value, there, n) for n in range(2)], axis=1)
+
         across = gather_end(i, first)
-        left = share(f"{i}0", share_start(f"{i}0", there(xs[0])))
+        left = share(f"{i}0", share_start(f"{i}0", forth(xs[0])))
         next(left)
         across.wait_recv()
-        right = share(f"{i}1", share_start(f"{i}1", there(xs[1])))
+        right = share(f"{i}1", share_start(f"{i}1", forth(xs[1])))
         meanwhile()
         next(right)
         for _ in range(2):
@@ -258,13 +267,15 @@
             next(right)
         for _ in left:
             pass
-        p[0] = three(dot, split(take(shared(f"{i}0"), 0)), pair(back))
+        value = split(take(shared(f"{i}0"), 0))
+        for c in range(p.shape[2] // 256):
+            p[0, :, 256 * c : 256 * c + 256] = product(dot, value, back, c)
         for _ in right:
             pass
         value, across = split(take(shared(f"{i}1"), 1)), []
         for c in range(p.shape[2] // 256):
             part = (slice(None), slice(256 * c, 256 * c + 256))
-            p[(1,) + part] = three(dot, value, (r_[back + "_h"][part], r_[back + "_l"][part]))
+            p[(1,) + part] = product(dot, value, back, c)
             across.append(copy(p.at[(1,) + part], cr.at[part], r_[f"cr{i}_s"].at[c], r_[f"cr{i}_r"].at[c], sibling))
         for c in across:
             c.wait_recv()
@@ -281,8 +292,11 @@
         return total
 
     first = gather_start(0)
+    loads["m1"].wait()
+    loads["m2"].wait()
+    index_one = order(r_["m1"][...], 256, "c1")
+    index_two = order(r_["m2"][...], 512, "c2")
     indices = to_owners("ti", index_one, index_two)
-    product = lambda dot_fn, name: lambda value: three(dot_fn, split(value), pair(name))
     eight = lambda value: jnp.concatenate([value, jnp.zeros((2, value.shape[1]), F32)], axis=0)
 
     for name in ("wc_h", "wc_l"):
@@ -302,7 +316,7 @@
             r_[n][0:192, 256:768] = jnp.zeros((192, 512), BF16)
             r_[n][192:512, 0:256] = jnp.zeros((320, 256), BF16)
 
-    updated = stage(0, first, product(dot_t, "wc"), prepare, lambda value, h: value, "kc")
+    updated = stage(0, first, "wc", prepare, lambda value, h: value, "kc")
     moved = to_owners("tu", eight(updated[:, 0:256]), eight(updated[:, 256:768]))
     for c in indices:
         c.wait_recv()
@@ -317,7 +331,7 @@
     first = gather_start(1)
     loads["ip"].wait()
     r_["wp_h"][...], r_["wp_l"][...] = split(r_["ip"][...])
-    parent = stage(1, first, product(dot_t, "wp"), lambda: None, lambda value, h: value, "wp")
+    parent = stage(1, first, "wp", lambda: None, lambda value, h: value, "wp")
     out[:, 1024:2048] = parent
 
     picked = exact(dot, eight(parent), "land")
@@ -330,7 +344,7 @@
     r_["ag2"][chip, :, 256:768] = exact(dot, pieces("tb", moved, 16, 48), "c2")[0:6]
     first = gather_start(2)
     reduced = lambda value, h: shared(f"0{h}") - value
-    out[:, 0:1024] = stage(2, first, product(dot_t, "kc"), lambda: None, reduced, "wc")
+    out[:, 0:1024] = stage(2, first, "kc", lambda: None, reduced, "wc")
 
     for c in sent:
         c.wait_send()

time: 165 us -> 165 us (level)
  no operation moved by 1% of the time
where the time goes in v4:
time: 165 us
  Pallas kernels  164 us (99%)
    pallas_call x1, Pallas kernels, local(): pl.pallas_call(kernel, name='fronts', out_shape=jax.ShapeDtypeStruct((6,...  163 us

profile of v4, /device:TPU:1, one launch (start us, length us, event | category | flops | bytes accessed | tf_op | source)
XLA Modules:
  0.0 165.0 jit_solution(16615579176908165654)
XLA Ops:
  0.6 162.9 %fronts.1.whole = f32[6,2048]{1,0:T(8,128)} custom-call(f32[6,384]{1,0:T(8,128)} %co.1, f32[6,640]{1,0:T(8,128)} %ct.1, f32[6,1024]{1,0:T(8,128)} %cp.1, f32[192,384]{1,0:T(8,128)} %io.1, f32[320,640]{1,0:T(8,128)} %it.1, f32[512,1024]{1,0:T(8,128)} %ip.1, f32[192,256]{1,0:T(8,128)} %ko.1, f32[320,512]{1,0:T(8,128)} %kt.1, s32[16,1,256]{2,1,0:T(1,128)} %bitcast.3, ...), custom_call_target="tpu_custom_call" | custom-call | tf_op jit(solution)/shard_map/fronts/pallas_call | solution.py:362
  163.5 1.5 parts.1
